TPU v7x, 128 devices: a whole 4x4x4 slice. The times are simulated.
128 devices in a mesh: pw: 32 (over x, z, y_hi), band: 4 (over y_lo, core).
Axes of the slice: x: 4, y: 4 (y_hi: 2, y_lo: 2; y = y_hi * 2 + y_lo), z: 4, core: 2. Of those that a mesh axis runs over, the one named last changes fastest.
Arguments:
- basis_set: bfloat16 [24576, 2048], P('pw'), may hold values from -0.078125 to 0.078125
- densities: bfloat16 [24576, 4096], P('pw', 'band'), may hold values from -135 to 135
- pair_gaps: float32 [4096], P('band'), may hold values from 0.002 to 500
- frequencies: float32 [16], replicated, may hold values from 0.01 to 100
Outputs:
- polarizability: float32 [16, 2048, 2048], P(None, 'pw', 'band')
- projected: bfloat16 [2048, 4096], P('pw', 'band')
All inputs are finite; a program needn't handle non-finite values.
Results may differ from a plain program's by a relative error of at most 0.011.
Values may be sent and summed in bfloat16 or wider, within the bound.
A program may use at most 128 MiB of HBM per device.

v0:
```python
import jax
import jax.numpy as jnp
from jax import lax
from jax.sharding import PartitionSpec as P

BATCH = 256
NBATCH = 4


def padded_to(lines, devices):
    spare = -lines.shape[0] % devices
    if not spare:
        return lines
    return jnp.concatenate([lines, jnp.zeros((spare, *lines.shape[1:]), lines.dtype)])


def from_everyone(value, axis):
    devices = lax.axis_size(axis)
    return lax.all_to_all(
        jnp.broadcast_to(value[None], (devices, *value.shape)), axis, 0, 0, tiled=True
    )


def laid_out(pieces, dim):
    shape = list(pieces.shape[1:])
    shape[dim] *= pieces.shape[0]
    return jnp.moveaxis(pieces, 0, dim).reshape(shape)


def gathered_copies(value, axis, dim):
    pieces = from_everyone(value, axis)
    return laid_out(pieces, dim)


def split_up(value, dim, devices):
    shape = value.shape
    pieces = value.reshape(*shape[:dim], devices, shape[dim] // devices, *shape[dim + 1 :])
    return jnp.moveaxis(pieces, dim, 0)


def sent_and_summed(value, axis, dim):
    devices = lax.axis_size(axis)
    pieces = lax.all_to_all(split_up(value, dim, devices), axis, 0, 0, tiled=True)
    return jnp.sum(pieces, axis=0)


def total_of(value, axes):
    lines = value.reshape(-1, value.shape[-1])
    padded = padded_to(lines, lax.axis_size(axes))
    whole = gathered_copies(sent_and_summed(padded, axes, 0), axes, 0)
    return lax.slice_in_dim(whole, 0, len(lines)).reshape(value.shape)


def weigh(gap_row, frequencies, pair_total):
    return (
        -4.0 / pair_total * gap_row[None, :] / (gap_row[None, :] ** 2 + frequencies[:, None] ** 2)
    )


def scale_rows(weights, own_rows):
    return (weights[:, None, :] * own_rows.astype(jnp.float32)[None, :, :]).astype(jnp.bfloat16)


def on_device(basis_set, densities, pair_gaps, frequencies):
    basis_width = basis_set.shape[1]
    pw_count = lax.axis_size("pw")
    band_count = lax.axis_size("band")
    row_share = basis_width // pw_count
    pair_total = pair_gaps.shape[0] * band_count
    nfreq = frequencies.shape[0]
    accumulated = jnp.zeros((nfreq, row_share, basis_width), jnp.float32)
    collected = []
    for position in range(NBATCH):
        dens_block = densities[:, position * BATCH : (position + 1) * BATCH]
        summed = total_of(
            lax.dot_general(
                basis_set, dens_block, (((0,), (0,)), ((), ())), preferred_element_type=jnp.float32
            ),
            "pw",
        )
        gathered = summed.astype(jnp.bfloat16)
        own_rows = lax.dynamic_slice_in_dim(
            gathered, lax.axis_index("pw") * row_share, row_share, 0
        )
        collected.append(own_rows)
        gap_row = pair_gaps[position * BATCH : (position + 1) * BATCH]
        scaled = scale_rows(weigh(gap_row, frequencies, pair_total), own_rows)
        accumulated = accumulated + jnp.einsum(
            "krp,cp->krc", scaled, gathered, preferred_element_type=jnp.float32
        )
    polarizability = lax.psum_scatter(
        accumulated.astype(jnp.bfloat16), "band", scatter_dimension=2, tiled=True
    ).astype(jnp.float32)
    projected = jnp.concatenate(collected, axis=1)
    return (polarizability, projected)


def solution(mesh):
    in_specs = (P("pw", None), P("pw", "band"), P("band"), P())
    out_specs = (P(None, "pw", "band"), P("pw", "band"))
    return jax.shard_map(
        on_device, mesh=mesh, in_specs=in_specs, out_specs=out_specs, check_vma=False
    )
```

profile of v0, /device:TPU:4, one launch (start us, length us, event | category | flops | bytes accessed | tf_op | source)
XLA Modules:
  0.0 336.3 jit_solution(9141219478820087704)
XLA Ops:
  7.2 0.0 copy-start
  7.2 1.9 copy-done
  9.1 3.3 fusion.15
  12.4 11.1 %all-to-all-start.2 = ((f32[32,64,256]{2,1,0:T(8,128)}), f32[32,64,256]{2,1,0:T(8,128)}, u32[]{:S(2)}, u32[]{:S(2)}) async-start(f32[32,64,256]{2,1,0:T(8,128)} %bitcast.27), calls=%async_computation.2 | async-start | bytes 4194304 | tf_op jit(solution)/shard_map/all_to_all | solution.py:43
  23.5 3.3 fusion.17
  26.9 24.1 %all-to-all-done.2 = f32[32,64,256]{2,1,0:T(8,128)} async-done(((f32[32,64,256]{2,1,0:T(8,128)}), f32[32,64,256]{2,1,0:T(8,128)}, u32[]{:S(2)}, u32[]{:S(2)}) %all-to-all-start.2) | async-done | bytes 2097184 | tf_op jit(solution)/shard_map/all_to_all | solution.py:43
  51.0 9.4 %all-to-all-start = ((f32[32,64,256]{2,1,0:T(8,128)}), f32[32,64,256]{2,1,0:T(8,128)}, u32[]{:S(2)}, u32[]{:S(2)}) async-start(f32[32,64,256]{2,1,0:T(8,128)} %bitcast.25), calls=%async_computation | async-start | bytes 4194304 | tf_op jit(solution)/shard_map/all_to_all | solution.py:43
  60.3 3.4 fusion.11
  63.7 24.2 %all-to-all-done = f32[32,64,256]{2,1,0:T(8,128)} async-done(((f32[32,64,256]{2,1,0:T(8,128)}), f32[32,64,256]{2,1,0:T(8,128)}, u32[]{:S(2)}, u32[]{:S(2)}) %all-to-all-start) | async-done | bytes 2097184 | tf_op jit(solution)/shard_map/all_to_all | solution.py:43
  87.9 9.1 %all-to-all-start.6 = ((f32[32,64,256]{2,1,0:T(8,128)}), f32[32,64,256]{2,1,0:T(8,128)}, u32[]{:S(2)}, u32[]{:S(2)}) async-start(f32[32,64,256]{2,1,0:T(8,128)} %bitcast.26), calls=%async_computation.6 | async-start | bytes 4194304 | tf_op jit(solution)/shard_map/all_to_all | solution.py:43
  97.1 3.3 fusion.13
  100.4 24.2 %all-to-all-done.6 = f32[32,64,256]{2,1,0:T(8,128)} async-done(((f32[32,64,256]{2,1,0:T(8,128)}), f32[32,64,256]{2,1,0:T(8,128)}, u32[]{:S(2)}, u32[]{:S(2)}) %all-to-all-start.6) | async-done | bytes 2097184 | tf_op jit(solution)/shard_map/all_to_all | solution.py:43
  124.7 9.1 %all-to-all-start.4 = ((f32[32,64,256]{2,1,0:T(8,128)}), f32[32,64,256]{2,1,0:T(8,128)}, u32[]{:S(2)}, u32[]{:S(2)}) async-start(f32[32,64,256]{2,1,0:T(8,128)} %bitcast.24), calls=%async_computation.4 | async-start | bytes 4194304 | tf_op jit(solution)/shard_map/all_to_all | solution.py:43
  133.8 1.7 reduce_sum.37
  135.5 25.9 %all-to-all-done.4 = f32[32,64,256]{2,1,0:T(8,128)} async-done(((f32[32,64,256]{2,1,0:T(8,128)}), f32[32,64,256]{2,1,0:T(8,128)}, u32[]{:S(2)}, u32[]{:S(2)}) %all-to-all-start.4) | async-done | bytes 2097184 | tf_op jit(solution)/shard_map/all_to_all | solution.py:43
  161.4 1.1 broadcast_in_dim.9
  162.5 9.1 %all-to-all-start.3 = ((bf16[32,64,256]{2,1,0:T(8,128)(2,1)}), bf16[32,64,256]{2,1,0:T(8,128)(2,1)}, u32[]{:S(2)}, u32[]{:S(2)}) async-start(bf16[32,64,256]{2,1,0:T(8,128)(2,1)} %broadcast_in_dim.9), calls=%async_computation.3 | async-start | bytes 2097152 | tf_op jit(solution)/shard_map/all_to_all | solution.py:19
  171.6 1.7 reduce_sum.36
  173.4 14.9 %all-to-all-done.3 = bf16[32,64,256]{2,1,0:T(8,128)(2,1)} async-done(((bf16[32,64,256]{2,1,0:T(8,128)(2,1)}), bf16[32,64,256]{2,1,0:T(8,128)(2,1)}, u32[]{:S(2)}, u32[]{:S(2)}) %all-to-all-start.3) | async-done | bytes 1048608 | tf_op jit(solution)/shard_map/all_to_all | solution.py:19
  188.3 1.1 broadcast_in_dim.8
  189.4 7.1 %all-to-all-start.1 = ((bf16[32,64,256]{2,1,0:T(8,128)(2,1)}), bf16[32,64,256]{2,1,0:T(8,128)(2,1)}, u32[]{:S(2)}, u32[]{:S(2)}) async-start(bf16[32,64,256]{2,1,0:T(8,128)(2,1)} %broadcast_in_dim.8), calls=%async_computation.1 | async-start | bytes 2097152 | tf_op jit(solution)/shard_map/all_to_all | solution.py:19
  196.5 1.7 reduce_sum.39
  198.2 14.1 %all-to-all-done.1 = bf16[32,64,256]{2,1,0:T(8,128)(2,1)} async-done(((bf16[32,64,256]{2,1,0:T(8,128)(2,1)}), bf16[32,64,256]{2,1,0:T(8,128)(2,1)}, u32[]{:S(2)}, u32[]{:S(2)}) %all-to-all-start.1) | async-done | bytes 1048608 | tf_op jit(solution)/shard_map/all_to_all | solution.py:19
  212.4 1.1 broadcast_in_dim.11
  213.4 7.1 %all-to-all-start.7 = ((bf16[32,64,256]{2,1,0:T(8,128)(2,1)}), bf16[32,64,256]{2,1,0:T(8,128)(2,1)}, u32[]{:S(2)}, u32[]{:S(2)}) async-start(bf16[32,64,256]{2,1,0:T(8,128)(2,1)} %broadcast_in_dim.11), calls=%async_computation.7 | async-start | bytes 2097152 | tf_op jit(solution)/shard_map/all_to_all | solution.py:19
  220.5 0.0 copy-start.2
  220.5 0.0 copy-start.1
  220.5 1.7 reduce_sum.38
  222.3 13.0 %all-to-all-done.7 = bf16[32,64,256]{2,1,0:T(8,128)(2,1)} async-done(((bf16[32,64,256]{2,1,0:T(8,128)(2,1)}), bf16[32,64,256]{2,1,0:T(8,128)(2,1)}, u32[]{:S(2)}, u32[]{:S(2)}) %all-to-all-start.7) | async-done | bytes 1048608 | tf_op jit(solution)/shard_map/all_to_all | solution.py:19
  235.3 1.1 broadcast_in_dim.10
  236.4 7.1 %all-to-all-start.5 = ((bf16[32,64,256]{2,1,0:T(8,128)(2,1)}), bf16[32,64,256]{2,1,0:T(8,128)(2,1)}, u32[]{:S(2)}, u32[]{:S(2)}) async-start(bf16[32,64,256]{2,1,0:T(8,128)(2,1)} %broadcast_in_dim.10), calls=%async_computation.5 | async-start | bytes 2097152 | tf_op jit(solution)/shard_map/all_to_all | solution.py:19
  243.5 0.2 reduce-scatter.2.cloned.1.call-start
  243.7 0.0 copy-done.2
  243.7 0.0 copy-done.1
  243.8 0.1 add_divide_fusion
  243.9 0.8 fusion.20
  244.6 0.8 fusion.21
  245.4 0.8 fusion.19
  246.2 11.7 %all-to-all-done.5 = bf16[32,64,256]{2,1,0:T(8,128)(2,1)} async-done(((bf16[32,64,256]{2,1,0:T(8,128)(2,1)}), bf16[32,64,256]{2,1,0:T(8,128)(2,1)}, u32[]{:S(2)}, u32[]{:S(2)}) %all-to-all-start.5) | async-done | bytes 1048608 | tf_op jit(solution)/shard_map/all_to_all | solution.py:19
  257.9 0.8 fusion.22
  258.7 2.5 fusion.2
  261.2 5.7 %fusion = f32[16,64,2048]{2,1,0:T(8,128)} fusion(bf16[2048,256,1]{1,0,2:T(8,128)(2,1)} %bitcast.2, f32[64,256]{1,0:T(8,128)S(1)} %get-tuple-element.6, f32[16,256]{1,0:T(8,128)S(1)} %get-tuple-element.21), kind=kOutput, calls=%fused_computation.5 | convolution fusion | flops 1074266112 | bytes 9519104 | tf_op jit(solution)/shard_map/krp,cp->krc/dot_general | solution.py:88
  266.9 5.7 %fusion.1 = f32[16,64,2048]{2,1,0:T(8,128)} fusion(bf16[2048,256,1]{1,0,2:T(8,128)(2,1)} %bitcast.5, f32[64,256]{1,0:T(8,128)S(1)} %get-tuple-element.4, f32[16,256]{1,0:T(8,128)S(1)} %get-tuple-element.19), kind=kOutput, calls=%fused_computation.6 | convolution fusion | flops 1074266112 | bytes 9519104 | tf_op jit(solution)/shard_map/krp,cp->krc/dot_general | solution.py:88
  272.7 9.4 %add_convert_fusion = bf16[16,64,2048]{2,1,0:T(8,128)(2,1)} fusion(f32[16,64,2048]{2,1,0:T(8,128)S(1)} %fusion.2, f32[16,64,2048]{2,1,0:T(8,128)} %fusion, f32[16,64,2048]{2,1,0:T(8,128)} %fusion.1, bf16[2048,256,1]{1,0,2:T(8,128)(2,1)} %bitcast.11, f32[64,256]{1,0:T(8,128)S(1)} %get-tuple-element.2, f32[16,256]{1,0:T(8,128)S(1)} %get-tuple-element.18), kind=kOutput, calls=%fused_computation | convolution fusion | flops 1082654720 | bytes 30490624 | tf_op jit(solution)/shard_map/krp,cp->krc/dot_general | solution.py:88
  282.1 0.0 reduce-scatter.2.cloned.1.call-update
  282.1 0.7 pad_maximum_fusion
  282.8 43.9 %reduce-scatter.2.cloned.1.call-done = bf16[16,64,512]{2,1,0:T(8,128)(2,1)} async-done(((bf16[16,64,2048]{2,1,0:T(8,128)(2,1)}), bf16[16,64,512]{2,1,0:T(8,128)(2,1)}) %reduce-scatter.2.cloned.1.call-update) | async-done | bytes 1048592 | tf_op jit(solution)/shard_map/reduce_scatter | solution.py:91
  326.7 2.8 convert_element_type.71
  (2 shorter events, 0.0 us)
Async XLA Ops:
  7.2 1.9 copy-start
  12.4 38.6 %all-to-all-start.2 = ((f32[32,64,256]{2,1,0:T(8,128)}), f32[32,64,256]{2,1,0:T(8,128)}, u32[]{:S(2)}, u32[]{:S(2)}) async-start(f32[32,64,256]{2,1,0:T(8,128)} %bitcast.27), calls=%async_computation.2 | async-start | bytes 4194304 | tf_op jit(solution)/shard_map/all_to_all | solution.py:43
  51.0 37.0 %all-to-all-start = ((f32[32,64,256]{2,1,0:T(8,128)}), f32[32,64,256]{2,1,0:T(8,128)}, u32[]{:S(2)}, u32[]{:S(2)}) async-start(f32[32,64,256]{2,1,0:T(8,128)} %bitcast.25), calls=%async_computation | async-start | bytes 4194304 | tf_op jit(solution)/shard_map/all_to_all | solution.py:43
  87.9 36.7 %all-to-all-start.6 = ((f32[32,64,256]{2,1,0:T(8,128)}), f32[32,64,256]{2,1,0:T(8,128)}, u32[]{:S(2)}, u32[]{:S(2)}) async-start(f32[32,64,256]{2,1,0:T(8,128)} %bitcast.26), calls=%async_computation.6 | async-start | bytes 4194304 | tf_op jit(solution)/shard_map/all_to_all | solution.py:43
  124.7 36.7 %all-to-all-start.4 = ((f32[32,64,256]{2,1,0:T(8,128)}), f32[32,64,256]{2,1,0:T(8,128)}, u32[]{:S(2)}, u32[]{:S(2)}) async-start(f32[32,64,256]{2,1,0:T(8,128)} %bitcast.24), calls=%async_computation.4 | async-start | bytes 4194304 | tf_op jit(solution)/shard_map/all_to_all | solution.py:43
  162.5 25.8 %all-to-all-start.3 = ((bf16[32,64,256]{2,1,0:T(8,128)(2,1)}), bf16[32,64,256]{2,1,0:T(8,128)(2,1)}, u32[]{:S(2)}, u32[]{:S(2)}) async-start(bf16[32,64,256]{2,1,0:T(8,128)(2,1)} %broadcast_in_dim.9), calls=%async_computation.3 | async-start | bytes 2097152 | tf_op jit(solution)/shard_map/all_to_all | solution.py:19
  189.4 23.0 %all-to-all-start.1 = ((bf16[32,64,256]{2,1,0:T(8,128)(2,1)}), bf16[32,64,256]{2,1,0:T(8,128)(2,1)}, u32[]{:S(2)}, u32[]{:S(2)}) async-start(bf16[32,64,256]{2,1,0:T(8,128)(2,1)} %broadcast_in_dim.8), calls=%async_computation.1 | async-start | bytes 2097152 | tf_op jit(solution)/shard_map/all_to_all | solution.py:19
  213.4 21.9 %all-to-all-start.7 = ((bf16[32,64,256]{2,1,0:T(8,128)(2,1)}), bf16[32,64,256]{2,1,0:T(8,128)(2,1)}, u32[]{:S(2)}, u32[]{:S(2)}) async-start(bf16[32,64,256]{2,1,0:T(8,128)(2,1)} %broadcast_in_dim.11), calls=%async_computation.7 | async-start | bytes 2097152 | tf_op jit(solution)/shard_map/all_to_all | solution.py:19
  220.5 23.2 %copy-start.2 = (f32[16]{0:T(128)S(1)}, f32[16]{0:T(128)}, u32[]{:S(2)}) copy-start(f32[16]{0:T(128)} %param.7) | copy-start | bytes 196
  220.5 23.2 %copy-start.1 = (f32[1024]{0:T(1024)S(1)}, f32[1024]{0:T(1024)}, u32[]{:S(2)}) copy-start(f32[1024]{0:T(1024)} %param.6) | copy-start | bytes 12292
  236.4 21.5 %all-to-all-start.5 = ((bf16[32,64,256]{2,1,0:T(8,128)(2,1)}), bf16[32,64,256]{2,1,0:T(8,128)(2,1)}, u32[]{:S(2)}, u32[]{:S(2)}) async-start(bf16[32,64,256]{2,1,0:T(8,128)(2,1)} %broadcast_in_dim.10), calls=%async_computation.5 | async-start | bytes 2097152 | tf_op jit(solution)/shard_map/all_to_all | solution.py:19
  243.5 83.2 %reduce-scatter.2.cloned.1.call-start = ((), (), s32[]{:S(2)}) async-start(), calls=%async_computation.9 | async-start | bytes 5242880 | tf_op jit(solution)/shard_map/reduce_scatter | solution.py:91
Sparse Core Ops, SparseCore 0:
  282.2 44.4 reduce-scatter.1
where the time goes:
time: 339 us; the launch traced here: 336 us
  waiting for transfers between devices  196 us (58%)
  starting transfers between devices  69.4 us (20%)
  matrix products  36.8 us (11%)
  between operations  14.2 us (4%)
  other arithmetic  13.6 us (4%)
  local copies, waits for them, and re-layouts  6.25 us (2%)
    all_to_all x4, waiting for transfers between devices, sent_and_summed(): lax.all_to_all(split_up(value, dim, devices), axis, 0, 0, tiled=True)  98.4 us
    all_to_all x4, waiting for transfers between devices, from_everyone(): lax.all_to_all(jnp.broadcast_to(value[None], (devices, *value.shape)), ax...  53.8 us
    reduce_scatter x1, waiting for transfers between devices, on_device(): lax.psum_scatter(accumulated.astype(jnp.bfloat16), 'band', scatter_dimens...  43.9 us
    all_to_all x4, starting transfers between devices, sent_and_summed(): lax.all_to_all(split_up(value, dim, devices), axis, 0, 0, tiled=True)  38.8 us
    all_to_all x4, starting transfers between devices, from_everyone(): lax.all_to_all(jnp.broadcast_to(value[None], (devices, *value.shape)), ax...  30.4 us
    dot_general x4, matrix products, on_device(): jnp.einsum('krp,cp->krc', scaled, gathered, preferred_element_type=jnp.fl...  23.4 us
    dot_general x4, matrix products, on_device(): lax.dot_general(basis_set, dens_block, (((0,), (0,)), ((), ())), preferre...  13.4 us
    reduce_sum x4, other arithmetic, sent_and_summed(): return jnp.sum(pieces, axis=0)  6.92 us
  transfers between devices with their start and end apart: 9, of which 9 were waited for; matrix products, arithmetic and copies ran while one was open for 6% of the time, Pallas kernels for 0%

commit v1 on v0

v1 whole, which is shorter than its diff:
```python
import functools

import jax
import jax.numpy as jnp
from jax import lax
from jax.experimental import pallas as pl
from jax.experimental.pallas import tpu as pltpu
from jax.sharding import PartitionSpec as P

MESH = pl.DeviceIdType.MESH
F32, BF16 = jnp.float32, jnp.bfloat16

NK = 768
NB = 2048
NP = 1024
NFREQ = 16
PAIRS = 4096
NBT = 2
W = NP // NBT
H = W // 2
Q = W // 4
NSEM = 96


def device(x, z, yh, yl, c):
    return ((x * 4 + z) * 2 + yh, yl * 2 + c)


def kernel(
    basis_hbm, dens_hbm, gaps, freq,
    pol, proj,
    basis, dens, bt,
    own_f32, s1_recv, s1_far, s1_near, s1_sum,
    s2_send, s2_recv,
    t_send, t_recv, y_send, y_recv,
    ib, gap_all, wts, scaled, jb,
    load_sem, send_sem, recv_sem, home_sem,
):
    pw, g = lax.axis_index("pw"), lax.axis_index("band")
    x, z, yh = pw // 8, (pw // 2) % 4, pw % 2
    yl, c = g // 2, g % 2
    me8 = yh * 4 + g

    loads = [
        pltpu.make_async_copy(basis_hbm, basis, load_sem.at[0]),
        pltpu.make_async_copy(dens_hbm, dens, load_sem.at[1]),
    ]
    for load in loads:
        load.start()

    def along(axis, d):
        if axis == "x":
            return device((x + d) % 4, z, yh, yl, c)
        return device(x, (z + d) % 4, yh, yl, c)

    def beside(d):
        o = (me8 + d) % 8
        return device(x, z, o // 4, (o % 4) // 2, o % 2)

    barrier = pltpu.get_barrier_semaphore()
    peers = [along(a, d) for a in "xz" for d in (1, 2, 3)] + [beside(d) for d in range(1, 8)]
    for peer in peers:
        pl.semaphore_signal(barrier, inc=1, device_id=peer, device_id_type=MESH)
    pl.semaphore_wait(barrier, len(peers))

    drains = []
    count = [0]

    def slot():
        count[0] += 1
        assert count[0] <= NSEM
        return count[0] - 1

    def copy_to(src, dst, sem, to, recv=None):
        return pltpu.make_async_remote_copy(
            src_ref=src, dst_ref=dst, send_sem=send_sem.at[sem],
            recv_sem=recv_sem.at[sem] if recv is None else recv,
            device_id=to, device_id_type=MESH,
        )

    def send(src, dst, sem, to, recv=None):
        cp = copy_to(src, dst, sem, to, recv)
        cp.start()
        drains.append((None, cp))
        return cp

    def send_if(cond, src, dst, sem, to, recv=None):
        cp = copy_to(src, dst, sem, to, recv)
        pl.when(cond)(cp.start)
        drains.append((cond, cp))
        return cp

    gap_all[g] = gaps[...]
    gap_sems = [slot() for _ in range(3)]
    gap_copies = []
    for d in range(1, 4):
        o = (g + d) % 4
        gap_copies.append(
            send(gaps, gap_all.at[g], gap_sems[d - 1], device(x, z, yh, o // 2, o % 2))
        )

    loads[0].wait()
    for i in range(16):
        bt[i // 4, i % 4] = basis[:, i * 128 : (i + 1) * 128].T
    loads[1].wait()

    def block(axis, q, lo, width):
        rows = bt[q] if axis == "x" else bt[:, q]
        return jnp.dot(
            rows.reshape(512, NK), dens[:, lo : lo + width], preferred_element_type=F32
        )

    here = {"x": x, "z": z}
    sem1 = {}

    def first_start(b, axis):
        h = 0 if axis == "x" else 1
        me, lo = here[axis], b * W + h * H
        sems = [slot() for _ in range(6)]
        sem1[b, axis] = sems
        far, near = s1_far.at[b, h], s1_near.at[b, h]
        value = block(axis, (me + 2) % 4, lo, H).astype(BF16)
        far[0] = value[:, :Q]
        far[1] = value[:, Q:]
        recv = s1_recv.at[b, h]
        copies = [
            send(far.at[0], recv.at[0], sems[0], along(axis, 1)),
            send(far.at[1], recv.at[1], sems[1], along(axis, 3)),
        ]
        value = block(axis, (me + 1) % 4, lo, H)
        near[1] = value[:, Q:].astype(BF16)
        copies.append(send(near.at[1], recv.at[3], sems[3], along(axis, 1)))
        own_f32[b, h, 0] = value[:, :Q]
        value = block(axis, (me + 3) % 4, lo, H)
        near[2] = value[:, :Q].astype(BF16)
        copies.append(send(near.at[2], recv.at[4], sems[4], along(axis, 3)))
        own_f32[b, h, 1] = value[:, Q:]
        sem1[b, axis] = (sems, copies)

    def first_own(b, axis):
        h = 0 if axis == "x" else 1
        me, lo = here[axis], b * W + h * H
        s1_sum[b, h] = block(axis, me, lo, H)

    def first_forward(b, axis):
        h = 0 if axis == "x" else 1
        sems, copies = sem1[b, axis]
        near, recv = s1_near.at[b, h], s1_recv.at[b, h]
        copies[0].wait_recv()
        near[0] = (own_f32[b, h, 0] + recv[0].astype(F32)).astype(BF16)
        copies.append(send(near.at[0], recv.at[2], sems[2], along(axis, 1)))
        copies[1].wait_recv()
        near[3] = (own_f32[b, h, 1] + recv[1].astype(F32)).astype(BF16)
        copies.append(send(near.at[3], recv.at[5], sems[5], along(axis, 3)))

    def first_end(b, axis):
        h = 0 if axis == "x" else 1
        recv = s1_recv.at[b, h]
        for cp in sem1[b, axis][1][2:]:
            cp.wait_recv()
        total = s1_sum.at[b, h]
        total[:, :Q] = total[:, :Q] + recv[2].astype(F32) + recv[4].astype(F32)
        total[:, Q:] = total[:, Q:] + recv[3].astype(F32) + recv[5].astype(F32)

    sem2 = {}

    def second_start(b, axis):
        h = 0 if axis == "x" else 1
        other = "z" if axis == "x" else "x"
        me = here[other]
        sems = [slot() for _ in range(3)]
        copies = []
        for i, d in enumerate((2, 1, 3)):
            start = pl.multiple_of((me + d) % 4 * 128, 128)
            s2_send[b, h, i] = s1_sum[b, h, pl.ds(start, 128), :].astype(BF16)
            copies.append(
                send(s2_send.at[b, h, i], s2_recv.at[b, h, i], sems[i], along(other, d))
            )
        sem2[b, axis] = copies

    def second_end(b, axis):
        h = 0 if axis == "x" else 1
        other = "z" if axis == "x" else "x"
        for cp in sem2[b, axis]:
            cp.wait_recv()
        start = pl.multiple_of(here[other] * 128, 128)
        total = s1_sum[b, h, pl.ds(start, 128), :]
        for i in range(3):
            total = total + s2_recv[b, h, i].astype(F32)
        t_send[b, :, h * H : (h + 1) * H] = total.astype(BF16)
        own = pl.multiple_of(yh * 64, 64)
        s1_sum[b, h, pl.ds(0, 128), :] = total
        y_send[b, :, h * H : (h + 1) * H] = s1_sum[
            b, h, pl.ds(pl.multiple_of((1 - yh) * 64, 64), 64), :
        ].astype(BF16)
        s1_sum[b, h, pl.ds(128, 64), :] = s1_sum[b, h, pl.ds(own, 64), :]

    is_home = g == x
    plane = yl * 2 + c
    step = 1 - 2 * (plane % 2)
    rel = (x - plane + 4) % 4
    is_source = rel == 0
    is_out1 = rel == (4 - step) % 4
    pair_to = device((plane + step + 4) % 4, z, yh, yl, c)
    out1_to = device((plane - step + 4) % 4, z, yh, yl, c)
    out2_to = device((plane + 2) % 4, z, yh, yl, c)

    sem_y = {}

    def third_start(b):
        homes = []
        for t in range(2):
            sem = slot()
            target8 = t * 4 + x
            mine = me8 == target8
            send_if(
                jnp.logical_not(mine), t_send.at[b], t_recv.at[b, me8], sem,
                device(x, z, t, x // 2, x % 2), recv=home_sem.at[b, me8],
            )

            @pl.when(mine)
            def _():
                t_recv[b, me8] = t_send[b]

        sem = slot()
        sem_y[b] = send(y_send.at[b], y_recv.at[b], sem, beside(4))

    sem_i = {}

    def rows_start(b):
        sem_y[b].wait_recv()
        for h in range(2):
            sl = slice(h * H, (h + 1) * H)
            value = s1_sum[b, h, pl.ds(128, 64), :] + y_recv[b, :, sl].astype(F32)
            proj[:, b * W + h * H : b * W + (h + 1) * H] = value.astype(BF16)
            ib[b, g, :, sl] = value.astype(BF16)
        copies = []
        for d in range(1, 4):
            o = (g + d) % 4
            sem = slot()
            copies.append(
                send(ib.at[b, g], ib.at[b, g], sem, device(x, z, yh, o // 2, o % 2))
            )
        sem_i[b] = copies

    def weigh(b):
        if b == 0:
            for cp in gap_copies:
                cp.wait_recv()
        square = freq[...] * freq[...]
        for gg in range(4):
            gap = gap_all[gg, :, b * W : (b + 1) * W]
            wts[b, gg // 2, :, (gg % 2) * W : (gg % 2 + 1) * W] = (
                (-4.0 / PAIRS) * gap / (gap * gap + square)
            )

    def scale(b):
        for cp in sem_i[b]:
            cp.wait_recv()
        for h in range(2):
            for e in range(2):
                sl = slice(e * W, (e + 1) * W)
                rows = ib[b, 2 * h + e].astype(F32)

                def at(k, _, h=h, sl=sl, rows=rows):
                    start = pl.multiple_of(k * 64, 64)
                    scaled[b, h, pl.ds(start, 64), sl] = (
                        wts[b, h, pl.ds(k, 1), sl] * rows
                    ).astype(BF16)
                    return 0

                lax.fori_loop(0, NFREQ, at, 0)

    sem_g = {}
    zn = [z, (z + 3) % 4, (z + 1) % 4, (z + 2) % 4]

    def wait_in(dst, sem, to):
        copy_to(dst, dst, sem, to).wait_recv()

    def gather1(b):
        ss = {name: slot() for name in ("x1", "x1o", "a1", "b1", "c1", "d1", "a2", "b2", "c2", "d2")}
        for i in range(4):
            ss["x2", i] = slot()
            ss["x2o", i] = slot()
        sem_g[b] = ss

        @pl.when(is_home)
        def _():
            for d in range(1, 8):
                o = (me8 + d) % 8
                copy_to(
                    t_recv.at[b, o], t_recv.at[b, o], 0, along("x", 1),
                    recv=home_sem.at[b, o],
                ).wait_recv()
            for gg in range(4):
                total = t_recv[b, gg].astype(F32) + t_recv[b, 4 + gg].astype(F32)
                jb[b, z, gg // 2, :, (gg % 2) * W : (gg % 2 + 1) * W] = total.astype(BF16)

        one, two = jb.at[b, z, 0], jb.at[b, z, 1]
        send_if(is_source, one, one, ss["x1"], out1_to)
        send_if(is_source, two, two, ss["a2"], along("z", 1))
        send_if(is_source, two, two, ss["b2"], along("z", 3))
        send_if(is_source, one, one, ss["x1o"], pair_to, recv=recv_sem.at[ss["x1"]])

    def gather2(b):
        ss = sem_g[b]
        one, two = jb.at[b, z, 0], jb.at[b, z, 1]

        @pl.when(jnp.logical_not(is_source))
        def _():
            wait_in(one, ss["x1"], along("x", 1))

        fwd = copy_to(one, one, ss["x1"], out2_to)
        pl.when(is_out1)(fwd.start)
        drains.append((is_out1, fwd))
        send(one, one, ss["a1"], along("z", 1))
        send(one, one, ss["b1"], along("z", 3))
        spread2(b, 0)

    def spread2(b, i):
        ss = sem_g[b]
        part = jb.at[b, zn[i], 1]
        send_if(is_source, part, part, ss["x2", i], out1_to)
        send_if(is_source, part, part, ss["x2o", i], pair_to, recv=recv_sem.at[ss["x2", i]])

    def pass2(b, i):
        ss = sem_g[b]
        part = jb.at[b, zn[i], 1]

        @pl.when(jnp.logical_not(is_source))
        def _():
            wait_in(part, ss["x2", i], along("x", 1))

        fwd = copy_to(part, part, ss["x2", i], out2_to)
        pl.when(is_out1)(fwd.start)
        drains.append((is_out1, fwd))

    def ring_mid(b, h, cond):
        ss = sem_g[b]
        n = str(h + 1)

        def go():
            wait_in(jb.at[b, zn[1], h], ss["a" + n], along("z", 1))

        def go2():
            wait_in(jb.at[b, zn[2], h], ss["b" + n], along("z", 1))

        lower, upper = jb.at[b, zn[1], h, pl.ds(0, 64)], jb.at[b, zn[2], h, pl.ds(64, 64)]
        if cond is None:
            go()
            send(lower, lower, ss["c" + n], along("z", 1))
            go2()
            send(upper, upper, ss["d" + n], along("z", 3))
        else:
            pl.when(cond)(go)
            send_if(cond, lower, lower, ss["c" + n], along("z", 1))
            pl.when(cond)(go2)
            send_if(cond, upper, upper, ss["d" + n], along("z", 3))

    def ring_end(b, h, cond):
        ss = sem_g[b]
        n = str(h + 1)

        def go():
            wait_in(jb.at[b, zn[3], h, pl.ds(0, 64)], ss["c" + n], along("z", 1))
            wait_in(jb.at[b, zn[3], h, pl.ds(64, 64)], ss["d" + n], along("z", 1))

        if cond is None:
            go()
        else:
            pl.when(cond)(go)

    def gather3(b):
        ring_mid(b, 1, is_source)
        spread2(b, 1)
        spread2(b, 2)
        ring_mid(b, 0, None)
        pass2(b, 0)

    def gather4(b):
        ring_end(b, 1, is_source)
        spread2(b, 3)
        pass2(b, 1)
        pass2(b, 2)

    def gather5(b):
        ring_end(b, 0, None)
        pass2(b, 3)

    def multiply(b, h, i, first=False):
        col = pl.multiple_of(zn[i] * 128, 128)
        value = lax.dot_general(
            scaled[b, h], jb[b, zn[i], h], (((1,), (1,)), ((), ())), preferred_element_type=F32
        )
        if first:
            pol[:, pl.ds(col, 128)] = value
        else:
            pol[:, pl.ds(col, 128)] += value

    batches = range(NBT)
    for b in batches:
        for axis in "xz":
            first_start(b, axis)
    for b in batches:
        for axis in "xz":
            first_forward(b, axis)
    for b in batches:
        for axis in "xz":
            first_own(b, axis)
    for b in batches:
        for axis in "xz":
            first_end(b, axis)
            second_start(b, axis)
        weigh(b)
    for b in batches:
        for axis in "xz":
            second_end(b, axis)
        third_start(b)
    for b in batches:
        gather1(b)
        rows_start(b)
        gather2(b)
    for b in batches:
        gather3(b)
        scale(b)
    for b in batches:
        gather4(b)
        for i in range(3):
            multiply(b, 0, i, first=b == 0)
        for i in range(3):
            multiply(b, 1, i)
    for b in batches:
        gather5(b)
        multiply(b, 0, 3, first=b == 0)
        multiply(b, 1, 3)

    for cond, cp in drains:
        if cond is None:
            cp.wait_send()
        else:
            pl.when(cond)(cp.wait_send)


def on_device(basis_set, densities, pair_gaps, frequencies):
    any_, vmem = pl.BlockSpec(memory_space=pl.ANY), pl.BlockSpec(memory_space=pltpu.VMEM)
    pol, proj = pl.pallas_call(
        kernel,
        out_shape=(
            jax.ShapeDtypeStruct((NFREQ * 64, 512), F32),
            jax.ShapeDtypeStruct((64, NP), BF16),
        ),
        in_specs=[any_, any_, vmem, vmem],
        out_specs=(vmem, vmem),
        scratch_shapes=[
            pltpu.VMEM((NK, NB), BF16),
            pltpu.VMEM((NK, NP), BF16),
            pltpu.VMEM((4, 4, 128, NK), BF16),
            pltpu.VMEM((NBT, 2, 2, 512, Q), F32),
            pltpu.VMEM((NBT, 2, 6, 512, Q), BF16),
            pltpu.VMEM((NBT, 2, 2, 512, Q), BF16),
            pltpu.VMEM((NBT, 2, 4, 512, Q), BF16),
            pltpu.VMEM((NBT, 2, 512, H), F32),
            pltpu.VMEM((NBT, 2, 3, 128, H), BF16),
            pltpu.VMEM((NBT, 2, 3, 128, H), BF16),
            pltpu.VMEM((NBT, 128, W), BF16),
            pltpu.VMEM((NBT, 8, 128, W), BF16),
            pltpu.VMEM((NBT, 64, W), BF16),
            pltpu.VMEM((NBT, 64, W), BF16),
            pltpu.VMEM((NBT, 4, 64, W), BF16),
            pltpu.VMEM((4, 1, NP), F32),
            pltpu.VMEM((NBT, 2, NFREQ, 2 * W), F32),
            pltpu.VMEM((NBT, 2, NFREQ * 64, 2 * W), BF16),
            pltpu.VMEM((NBT, 4, 2, 128, 2 * W), BF16),
            pltpu.SemaphoreType.DMA((2,)),
            pltpu.SemaphoreType.DMA((NSEM,)),
            pltpu.SemaphoreType.DMA((NSEM,)),
            pltpu.SemaphoreType.DMA((NBT, 8)),
        ],
        compiler_params=pltpu.CompilerParams(
            collective_id=0, has_side_effects=True, vmem_limit_bytes=56 * 2**20
        ),
    )(basis_set, densities, pair_gaps.reshape(1, NP), frequencies.reshape(NFREQ, 1))
    return pol.reshape(NFREQ, 64, 512), proj


def solution(mesh):
    in_specs = (P("pw", None), P("pw", "band"), P("band"), P())
    out_specs = (P(None, "pw", "band"), P("pw", "band"))
    return jax.shard_map(
        on_device, mesh=mesh, in_specs=in_specs, out_specs=out_specs, check_vma=False
    )
```

time: 339 us -> 97.4 us (0.29)
  waiting for transfers between devices: 196 us -> 0 us
  Pallas kernels: 0 us -> 91.3 us
  starting transfers between devices: 69.4 us -> 0 us
  matrix products: 36.8 us -> 0 us
  other arithmetic: 13.6 us -> 0 us
  between operations: 14.2 us -> 0.65 us
    all_to_all x8 -> x0, waiting for transfers between devices: 152 us -> none  [the longest x4 98.4 us: sent_and_summed(): lax.all_to_all(split_up(value, dim, devices), axis, 0, 0, tiled=True)]
    pallas_call x0 -> x1, Pallas kernels: none -> 91.3 us  [on_device(): pl.pallas_call(kernel, out_shape=(jax.ShapeDtypeStruct((NFREQ * 64, 512),...]
    all_to_all x8 -> x0, starting transfers between devices: 69.2 us -> none  [the longest x4 38.8 us: sent_and_summed(): lax.all_to_all(split_up(value, dim, devices), axis, 0, 0, tiled=True)]
    reduce_scatter x1 -> x0, waiting for transfers between devices: 43.9 us -> none  [on_device(): lax.psum_scatter(accumulated.astype(jnp.bfloat16), 'band', scatter_dimens...]
    dot_general x8 -> x0, matrix products: 36.8 us -> none  [the longest x4 23.4 us: on_device(): jnp.einsum('krp,cp->krc', scaled, gathered, preferred_element_type=jnp.fl...]
    reduce_sum x4 -> x0, other arithmetic: 6.92 us -> none  [sent_and_summed(): return jnp.sum(pieces, axis=0)]
    convert_element_type x5 -> x0, other arithmetic: 5.89 us -> none  [the longest x4 3.07 us: scale_rows(): own_rows.astype(jnp.float32)[None, :, :]]
    broadcast_in_dim x4 -> x0, local copies, waits for them, and re-layouts: 4.35 us -> none  [from_everyone(): jnp.broadcast_to(value[None], (devices, *value.shape))]
  transfers between devices with their start and end apart: 9 -> 0, of which waited for: 9 -> 0; matrix products, arithmetic and copies ran while one was open for 6% -> 0% of each run, Pallas kernels for 0% -> 0%
where the time goes in v1:
time: 97.4 us; the launch traced here: 97.2 us
  Pallas kernels  91.3 us (94%)
  local copies, waits for them, and re-layouts  5.17 us (5%)
    pallas_call x1, Pallas kernels, on_device(): pl.pallas_call(kernel, out_shape=(jax.ShapeDtypeStruct((NFREQ * 64, 512),...  91.3 us
    unnamed x4, local copies, waits for them, and re-layouts  3.84 us

profile of v1, /device:TPU:4, one launch (start us, length us, event | category | flops | bytes accessed | tf_op | source)
XLA Modules:
  0.0 97.2 jit_solution(18294124920455789280)
XLA Ops:
  0.6 1.3 %copy.6.freq = f32[16,1]{1,0:T(8,128)} copy(f32[16,1]{0,1:T(1,128)} %bitcast.5) | data formatting | bytes 128 | tf_op jit(solution)/shard_map/reshape | solution.py:482
  2.0 91.3 %shard_map.59 = (f32[1024,512]{1,0:T(8,128)}, bf16[64,1024]{1,0:T(8,128)(2,1)}) custom-call(bf16[768,2048]{1,0:T(8,128)(2,1)} %basis_hbm.1, bf16[768,1024]{1,0:T(8,128)(2,1)} %dens_hbm.1, f32[1,1024]{1,0:T(1,128)} %bitcast.4, f32[16,1]{1,0:T(8,128)} %copy.6.freq), custom_call_target="tpu_custom_call" | custom-call | tf_op jit(solution)/shard_map/pallas_call | solution.py:446
  93.3 0.0 copy-start
  93.3 3.2 %copy.9 = f32[16,64,512]{2,1,0:T(8,128)} copy(f32[16,64,512]{2,1,0:T(8,128)} %bitcast.3) | data formatting | bytes 4194304
  96.5 0.0 copy-done
  96.5 0.7 copy.10
Async XLA Ops:
  93.3 3.2 %copy-start = (bf16[64,1024]{1,0:T(8,128)(2,1)S(1)}, bf16[64,1024]{1,0:T(8,128)(2,1)}, u32[]{:S(2)}) copy-start(bf16[64,1024]{1,0:T(8,128)(2,1)} %get-tuple-element.9) | copy-start | bytes 393220

commit v2 on v1

v2 whole, which is shorter than its diff:
```python
import functools

import jax
import jax.numpy as jnp
from jax import lax
from jax.experimental import pallas as pl
from jax.experimental.pallas import tpu as pltpu
from jax.sharding import PartitionSpec as P

MESH = pl.DeviceIdType.MESH
F32, BF16 = jnp.float32, jnp.bfloat16

NK = 768
NB = 2048
NP = 1024
NFREQ = 16
PAIRS = 4096
NBT = 2
W = NP // NBT
H = W // 2
Q = W // 4
NSEM = 160


def device(x, z, yh, yl, c):
    return ((x * 4 + z) * 2 + yh, yl * 2 + c)


def kernel(
    basis_hbm, dens_hbm, gaps, freq,
    pol, proj,
    basis, dens, bt,
    own_f32, s1_recv, s1_far, s1_near, s1_sum,
    s2_send, s2_recv,
    t_own, y_send, y_recv,
    ib, gap_all, wts, scaled, jb,
    load_sem, send_sem, recv_sem, home_sem, row_sem,
):
    pw, g = lax.axis_index("pw"), lax.axis_index("band")
    x, z, yh = pw // 8, (pw // 2) % 4, pw % 2
    yl, c = g // 2, g % 2
    me8 = yh * 4 + g

    def fetch(src, dst, cols, n):
        return pltpu.make_async_copy(src.at[:, cols], dst.at[:, cols], load_sem.at[n])

    loads = [fetch(dens_hbm, dens, pl.ds(0, W), 0)]
    for n, d in enumerate((2, 0, 1, 3)):
        cols = pl.ds(pl.multiple_of((x + d) % 4 * 512, 512), 512)
        loads.append(fetch(basis_hbm, basis, cols, n + 1))
    loads.append(fetch(dens_hbm, dens, pl.ds(W, NP - W), 5))
    for load in loads:
        load.start()

    def along(axis, d):
        if axis == "x":
            return device((x + d) % 4, z, yh, yl, c)
        return device(x, (z + d) % 4, yh, yl, c)

    def beside(d):
        o = (me8 + d) % 8
        return device(x, z, o // 4, (o % 4) // 2, o % 2)

    barrier = pltpu.get_barrier_semaphore()
    peers = [along(a, d) for a in "xz" for d in (1, 2, 3)] + [beside(d) for d in range(1, 8)]
    for peer in peers:
        pl.semaphore_signal(barrier, inc=1, device_id=peer, device_id_type=MESH)
    pl.semaphore_wait(barrier, len(peers))

    drains = []
    count = [0]

    def slot():
        count[0] += 1
        assert count[0] <= NSEM
        return count[0] - 1

    def copy_to(src, dst, sem, to, recv=None):
        return pltpu.make_async_remote_copy(
            src_ref=src, dst_ref=dst, send_sem=send_sem.at[sem],
            recv_sem=recv_sem.at[sem] if recv is None else recv,
            device_id=to, device_id_type=MESH,
        )

    def send(src, dst, sem, to, recv=None):
        cp = copy_to(src, dst, sem, to, recv)
        cp.start()
        drains.append((None, cp))
        return cp

    def send_if(cond, src, dst, sem, to, recv=None):
        cp = copy_to(src, dst, sem, to, recv)
        pl.when(cond)(cp.start)
        drains.append((cond, cp))
        return cp

    gap_all[g] = gaps[...]
    gap_sems = [slot() for _ in range(3)]
    gap_copies = []
    for d in range(1, 4):
        o = (g + d) % 4
        gap_copies.append(
            send(gaps, gap_all.at[g], gap_sems[d - 1], device(x, z, yh, o // 2, o % 2))
        )

    def turn(i, j):
        start = pl.multiple_of((i * 4 + j) * 128, 128)
        bt[i, j] = basis[:, pl.ds(start, 128)].T

    loads[0].wait()
    loads[1].wait()
    for j in range(4):
        turn((x + 2) % 4, j)

    def block(axis, q, lo, width):
        rows = bt[q] if axis == "x" else bt[:, q]
        return jnp.dot(
            rows.reshape(512, NK), dens[:, lo : lo + width], preferred_element_type=F32
        )

    here = {"x": x, "z": z}
    sem1 = {}

    def first_start(b, axis):
        h = 0 if axis == "x" else 1
        me, lo = here[axis], b * W + h * H
        sems = [slot() for _ in range(6)]
        far, near = s1_far.at[b, h], s1_near.at[b, h]
        if b == 1 and axis == "x":
            loads[5].wait()
        if b == 0 and axis == "z":
            for n, d in enumerate((0, 1, 3)):
                loads[n + 2].wait()
                turn((x + d) % 4, (z + 2) % 4)
        value = block(axis, (me + 2) % 4, lo, H).astype(BF16)
        far[0] = value[:, :Q]
        far[1] = value[:, Q:]
        recv = s1_recv.at[b, h]
        copies = [
            send(far.at[0], recv.at[0], sems[0], along(axis, 1)),
            send(far.at[1], recv.at[1], sems[1], along(axis, 3)),
        ]
        sem1[b, axis] = (sems, copies)

    def near_part(b, axis):
        h = 0 if axis == "x" else 1
        me, lo = here[axis], b * W + h * H
        sems, copies = sem1[b, axis]
        near, recv = s1_near.at[b, h], s1_recv.at[b, h]
        value = block(axis, (me + 1) % 4, lo, H)
        near[1] = value[:, Q:].astype(BF16)
        copies.append(send(near.at[1], recv.at[3], sems[3], along(axis, 1)))
        own_f32[b, h, 0] = value[:, :Q]
        value = block(axis, (me + 3) % 4, lo, H)
        near[2] = value[:, :Q].astype(BF16)
        copies.append(send(near.at[2], recv.at[4], sems[4], along(axis, 3)))
        own_f32[b, h, 1] = value[:, Q:]

    def first_own(b, axis):
        h = 0 if axis == "x" else 1
        me, lo = here[axis], b * W + h * H
        s1_sum[b, h] = block(axis, me, lo, H)

    def first_forward(b, axis):
        h = 0 if axis == "x" else 1
        sems, copies = sem1[b, axis]
        near, recv = s1_near.at[b, h], s1_recv.at[b, h]
        copies[0].wait_recv()
        near[0] = (own_f32[b, h, 0] + recv[0].astype(F32)).astype(BF16)
        copies.append(send(near.at[0], recv.at[2], sems[2], along(axis, 1)))
        copies[1].wait_recv()
        near[3] = (own_f32[b, h, 1] + recv[1].astype(F32)).astype(BF16)
        copies.append(send(near.at[3], recv.at[5], sems[5], along(axis, 3)))

    def first_end(b, axis):
        h = 0 if axis == "x" else 1
        recv = s1_recv.at[b, h]
        for cp in sem1[b, axis][1][2:]:
            cp.wait_recv()
        total = s1_sum.at[b, h]
        total[:, :Q] = total[:, :Q] + recv[2].astype(F32) + recv[4].astype(F32)
        total[:, Q:] = total[:, Q:] + recv[3].astype(F32) + recv[5].astype(F32)

    sem2 = {}

    def second_start(b, axis):
        h = 0 if axis == "x" else 1
        other = "z" if axis == "x" else "x"
        me = here[other]
        sems = [slot() for _ in range(3)]
        copies = []
        for i, d in enumerate((2, 1, 3)):
            start = pl.multiple_of((me + d) % 4 * 128, 128)
            s2_send[b, h, i] = s1_sum[b, h, pl.ds(start, 128), :].astype(BF16)
            copies.append(
                send(s2_send.at[b, h, i], s2_recv.at[b, h, i], sems[i], along(other, d))
            )
        sem2[b, axis] = copies

    is_home = g == x
    is_source = is_home
    step = 1 - 2 * (g % 2)
    rel = (x - g + 4) % 4
    is_out1 = rel == (4 - step) % 4
    pair_to = device((g + step + 4) % 4, z, yh, yl, c)
    out1_to = device((g - step + 4) % 4, z, yh, yl, c)
    out2_to = device((g + 2) % 4, z, yh, yl, c)

    def split(b):
        return b == 0

    sem_y = {}

    def second_end(b, axis):
        h = 0 if axis == "x" else 1
        other = "z" if axis == "x" else "x"
        for cp in sem2[b, axis]:
            cp.wait_recv()
        start = pl.multiple_of(here[other] * 128, 128)
        total = s1_sum[b, h, pl.ds(start, 128), :]
        for i in range(3):
            total = total + s2_recv[b, h, i].astype(F32)
        t_own[b, h] = total
        theirs = pl.multiple_of((1 - yh) * 64, 64)
        y_send[b, h] = t_own[b, h, pl.ds(theirs, 64), :].astype(BF16)
        sem_y[b, h] = send(y_send.at[b, h], y_recv.at[b, h], slot(), beside(4))

    own_rows = pl.ds(pl.multiple_of(yh * 64, 64), 64)

    def rows_start(b):
        for h in range(2):
            sem_y[b, h].wait_recv()
            value = (t_own[b, h, own_rows, :] + y_recv[b, h].astype(F32)).astype(BF16)
            proj[:, b * W + h * H : b * W + (h + 1) * H] = value
            ib[b, g, h] = value
        other_home = device(x, z, 1 - yh, x // 2, x % 2)
        for h in range(2):
            cond = yl != yh if h == 1 and split(b) else None
            pair = (ib.at[b, g, h], jb.at[b, z, h, g, own_rows])
            if cond is None:
                send(*pair, slot(), other_home, recv=home_sem.at[b, h, g])
            else:
                send_if(cond, *pair, slot(), other_home, recv=home_sem.at[b, h, g])
        mine = ib.at[b, g]
        send_if(
            g != x, mine, mine, slot(), device(x, z, yh, x // 2, x % 2),
            recv=row_sem.at[b, (x - g + 4) % 4],
        )

    def rows_more(b):
        mine = ib.at[b, g]
        for d in range(1, 4):
            o = (g + d) % 4
            send_if(
                o != x, mine, mine, slot(), device(x, z, yh, o // 2, o % 2),
                recv=row_sem.at[b, d],
            )

    def rows_end(b):
        for d in range(1, 4):
            o = (g - d + 4) % 4
            copy_to(ib.at[b, o], ib.at[b, o], 0, along("x", 1), recv=row_sem.at[b, d]).wait_recv()

    def weigh(b):
        if b == 0:
            for cp in gap_copies:
                cp.wait_recv()
        column = lax.broadcasted_iota(jnp.int32, (NFREQ, W), 0)
        square = jnp.zeros((NFREQ, W), F32)
        for k in range(NFREQ):
            square = jnp.where(column == k, freq[k] * freq[k], square)
        for gg in range(4):
            gap = gap_all[gg, :, b * W : (b + 1) * W]
            value = (-4.0 / PAIRS) * gap / (gap * gap + square)
            for h in range(2):
                wts[b, h, :, gg * H : (gg + 1) * H] = value[:, h * H : (h + 1) * H]

    def scale(b):
        pl.when(jnp.logical_not(is_home))(lambda: rows_end(b))
        for h in range(2):
            for gg in range(4):
                sl = slice(gg * H, (gg + 1) * H)
                rows = ib[b, gg, h].astype(F32)

                def at(k, _, h=h, sl=sl, rows=rows):
                    start = pl.multiple_of(k * 64, 64)
                    scaled[b, h, pl.ds(start, 64), sl] = (
                        wts[b, h, pl.ds(k, 1), sl] * rows
                    ).astype(BF16)
                    return 0

                lax.fori_loop(0, NFREQ, at, 0)

    sem_g = {}
    zn = [z, (z + 3) % 4, (z + 1) % 4, (z + 2) % 4]

    def wait_in(dst, sem, to):
        copy_to(dst, dst, sem, to).wait_recv()

    def part(b, zz, h):
        if h == 1 and split(b):
            return jb.at[b, zz, 1, pl.ds(2 * yh, 2)]
        return jb.at[b, zz, h]

    def half(b, zz, h, n):
        if h == 1 and split(b):
            return jb.at[b, zz, 1, pl.ds(2 * yh + n, 1)]
        return jb.at[b, zz, h, pl.ds(2 * n, 2)]

    def pieces(b, zz, h):
        if h == 1 and split(b):
            return [part(b, zz, h)]
        return [half(b, zz, h, n) for n in range(2)]

    def gather1(b):
        ss = {name + str(h): slot() for name in ("a0", "a1", "b0", "b1", "c", "d") for h in range(2)}
        for n in range(2):
            ss["x1", n] = slot()
            ss["x1o", n] = slot()
        for i in range(4):
            for n in range(1 if split(b) else 2):
                ss["x2", i, n] = slot()
                ss["x2o", i, n] = slot()
            if split(b):
                ss["y2", i] = slot()
        sem_g[b] = ss
        pl.when(is_home)(lambda: rows_end(b))
        for h in range(2):

            @pl.when(is_home)
            def _(h=h):
                groups = [2 * yh, 2 * yh + 1] if h == 1 and split(b) else range(4)
                for gg in groups:
                    jb[b, z, h, gg, own_rows, :] = ib[b, gg, h]
                for gg in groups:
                    block = jb.at[b, z, h, gg, own_rows]
                    copy_to(block, block, 0, along("x", 1), recv=home_sem.at[b, h, gg]).wait_recv()

            if h == 0:
                for n, piece in enumerate(pieces(b, z, 0)):
                    send_if(is_source, piece, piece, ss["x1", n], out1_to)
                    send_if(
                        is_source, piece, piece, ss["x1o", n], pair_to,
                        recv=recv_sem.at[ss["x1", n]],
                    )
            else:
                ring_start(b, 1, is_source)

    def ring_start(b, h, cond):
        ss = sem_g[b]
        for n in range(2):
            up, down = half(b, z, h, n), half(b, z, h, 1 - n)
            one = (up, up, ss[f"a{n}{h}"], along("z", 1))
            two = (down, down, ss[f"b{1 - n}{h}"], along("z", 3))
            for args in (one, two):
                if cond is None:
                    send(*args)
                else:
                    send_if(cond, *args)

    def gather2(b):
        ss = sem_g[b]
        for n, piece in enumerate(pieces(b, z, 0)):

            @pl.when(jnp.logical_not(is_source))
            def _(n=n, piece=piece):
                wait_in(piece, ss["x1", n], along("x", 1))

            fwd = copy_to(piece, piece, ss["x1", n], out2_to)
            pl.when(is_out1)(fwd.start)
            drains.append((is_out1, fwd))
        ring_start(b, 0, None)
        spread2(b, 0)

    def spread2(b, i, which=None):
        ss = sem_g[b]
        for n, piece in enumerate(pieces(b, zn[i], 1)):
            if which is None or n == which:
                send_if(is_source, piece, piece, ss["x2", i, n], out1_to)
                send_if(
                    is_source, piece, piece, ss["x2o", i, n], pair_to,
                    recv=recv_sem.at[ss["x2", i, n]],
                )

    def pass2(b, i):
        ss = sem_g[b]
        for n, piece in enumerate(pieces(b, zn[i], 1)):

            @pl.when(jnp.logical_not(is_source))
            def _(n=n, piece=piece):
                wait_in(piece, ss["x2", i, n], along("x", 1))

            fwd = copy_to(piece, piece, ss["x2", i, n], out2_to)
            pl.when(is_out1)(fwd.start)
            drains.append((is_out1, fwd))
        if split(b):
            send(piece, piece, ss["y2", i], beside(4))

    def across_end(b, i):
        wait_in(jb.at[b, zn[i], 1, pl.ds(2 - 2 * yh, 2)], sem_g[b]["y2", i], beside(4))

    def under(cond, go):
        if cond is None:
            go()
        else:
            pl.when(cond)(go)

    def ring_mid(b, h, cond):
        ss = sem_g[b]
        lower, upper = half(b, zn[1], h, 0), half(b, zn[2], h, 1)
        for ref, name, on, d in ((lower, "a0", "c", 1), (upper, "b1", "d", 3)):
            under(cond, lambda ref=ref, name=name: wait_in(ref, ss[f"{name}{h}"], along("z", 1)))
            if cond is None:
                send(ref, ref, ss[f"{on}{h}"], along("z", d))
            else:
                send_if(cond, ref, ref, ss[f"{on}{h}"], along("z", d))
        for i, n, name in ((1, 1, "a1"), (2, 0, "b0")):
            ref = half(b, zn[i], h, n)
            under(cond, lambda ref=ref, name=name: wait_in(ref, ss[f"{name}{h}"], along("z", 1)))

    def ring_end(b, h, cond, after=None):
        ss = sem_g[b]
        for n, name in enumerate("cd"):
            ref = half(b, zn[3], h, n)
            under(cond, lambda ref=ref, name=name: wait_in(ref, ss[f"{name}{h}"], along("z", 1)))
            if after is not None:
                after(n)

    def gather3(b):
        ring_mid(b, 1, is_source)
        spread2(b, 1)
        spread2(b, 2)
        ring_mid(b, 0, None)
        pass2(b, 0)

    def gather4(b):
        if split(b):
            ring_end(b, 1, is_source)
            spread2(b, 3)
        else:
            ring_end(b, 1, is_source, lambda n: spread2(b, 3, n))
        pass2(b, 1)
        pass2(b, 2)

    def gather5(b):
        ring_end(b, 0, None)
        pass2(b, 3)

    def multiply(b, h, which, first=False):
        if h == 1 and split(b):
            for i in which:
                across_end(b, i)
        rows = jnp.concatenate(
            [
                jnp.concatenate([jb[b, zn[i], h, gg] for gg in range(4)], axis=1)
                for i in which
            ],
            axis=0,
        )
        value = lax.dot_general(
            scaled[b, h], rows, (((1,), (1,)), ((), ())), preferred_element_type=F32
        )
        for n, i in enumerate(which):
            col = pl.ds(pl.multiple_of(zn[i] * 128, 128), 128)
            share = value[:, n * 128 : (n + 1) * 128]
            if first:
                pol[:, col] = share
            else:
                pol[:, col] += share

    first_start(0, 'x')
    first_start(0, 'z')
    for d in (0, 1, 3):
        for e in (0, 1, 3):
            turn((x + d) % 4, (z + e) % 4)
    near_part(0, 'x')
    near_part(0, 'z')
    first_start(1, 'x')
    first_start(1, 'z')
    first_own(0, 'x')
    first_own(0, 'z')
    first_forward(0, 'x')
    first_forward(0, 'z')
    near_part(1, 'x')
    near_part(1, 'z')
    first_own(1, 'x')
    first_own(1, 'z')
    first_end(0, 'x')
    first_end(0, 'z')
    second_start(0, 'x')
    second_start(0, 'z')
    first_forward(1, 'x')
    first_forward(1, 'z')
    weigh(0)
    weigh(1)
    second_end(0, 'x')
    second_end(0, 'z')
    first_end(1, 'x')
    first_end(1, 'z')
    second_start(1, 'x')
    second_start(1, 'z')
    rows_start(0)
    second_end(1, 'x')
    second_end(1, 'z')
    gather1(0)
    rows_start(1)
    gather2(0)
    rows_more(0)
    gather1(1)
    gather3(0)
    gather2(1)
    rows_more(1)
    gather4(0)
    scale(0)
    gather3(1)
    multiply(0, 0, (0, 1), first=True)
    gather5(0)
    scale(1)
    multiply(0, 0, (2, 3), first=True)
    gather4(1)
    multiply(0, 1, (0, 1))
    multiply(0, 1, (2, 3))
    multiply(1, 0, (0, 1))
    multiply(1, 1, (0, 1))
    gather5(1)
    multiply(1, 0, (2, 3))
    multiply(1, 1, (2, 3))
    for cond, cp in drains:
        if cond is None:
            cp.wait_send()
        else:
            pl.when(cond)(cp.wait_send)


def on_device(basis_set, densities, pair_gaps, frequencies):
    any_, vmem = pl.BlockSpec(memory_space=pl.ANY), pl.BlockSpec(memory_space=pltpu.VMEM)
    pol, proj = pl.pallas_call(
        kernel,
        out_shape=(
            pltpu.VMEM((NFREQ * 64, 512), F32),
            pltpu.VMEM((64, NP), BF16),
        ),
        in_specs=[any_, any_, vmem, pl.BlockSpec(memory_space=pltpu.SMEM)],
        out_specs=(vmem, vmem),
        scratch_shapes=[
            pltpu.VMEM((NK, NB), BF16),
            pltpu.VMEM((NK, NP), BF16),
            pltpu.VMEM((4, 4, 128, NK), BF16),
            pltpu.VMEM((NBT, 2, 2, 512, Q), F32),
            pltpu.VMEM((NBT, 2, 6, 512, Q), BF16),
            pltpu.VMEM((NBT, 2, 2, 512, Q), BF16),
            pltpu.VMEM((NBT, 2, 4, 512, Q), BF16),
            pltpu.VMEM((NBT, 2, 512, H), F32),
            pltpu.VMEM((NBT, 2, 3, 128, H), BF16),
            pltpu.VMEM((NBT, 2, 3, 128, H), BF16),
            pltpu.VMEM((NBT, 2, 128, H), F32),
            pltpu.VMEM((NBT, 2, 64, H), BF16),
            pltpu.VMEM((NBT, 2, 64, H), BF16),
            pltpu.VMEM((NBT, 4, 2, 64, H), BF16),
            pltpu.VMEM((4, 1, NP), F32),
            pltpu.VMEM((NBT, 2, NFREQ, 2 * W), F32),
            pltpu.VMEM((NBT, 2, NFREQ * 64, 2 * W), BF16),
            pltpu.VMEM((NBT, 4, 2, 4, 128, H), BF16),
            pltpu.SemaphoreType.DMA((6,)),
            pltpu.SemaphoreType.DMA((NSEM,)),
            pltpu.SemaphoreType.DMA((NSEM,)),
            pltpu.SemaphoreType.DMA((NBT, 2, 4)),
            pltpu.SemaphoreType.DMA((NBT, 4)),
        ],
        compiler_params=pltpu.CompilerParams(
            collective_id=0, has_side_effects=True, vmem_limit_bytes=56 * 2**20
        ),
    )(basis_set, densities, pair_gaps.reshape(1, NP), frequencies)
    return pol.reshape(NFREQ, 64, 512), proj


def solution(mesh):
    in_specs = (P("pw", None), P("pw", "band"), P("band"), P())
    out_specs = (P(None, "pw", "band"), P("pw", "band"))
    return jax.shard_map(
        on_device, mesh=mesh, in_specs=in_specs, out_specs=out_specs, check_vma=False
    )
```

time: 97.4 us -> 81.9 us (0.84)
  Pallas kernels: 91.3 us -> 79.1 us
  local copies, waits for them, and re-layouts: 5.17 us -> 1.98 us
    pallas_call x1, Pallas kernels: 91.3 us -> 79.1 us  [on_device(): pl.pallas_call(kernel, out_shape=(pltpu.VMEM((NFREQ * 64, 512), F32), plt...]
    unnamed x4 -> x2, local copies, waits for them, and re-layouts: 3.84 us -> 1.98 us
    reshape x1 -> x0, local copies, waits for them, and re-layouts: 1.33 us -> none  [on_device(): frequencies.reshape(NFREQ, 1)]
where the time goes in v2:
time: 81.9 us; the launch traced here: 81.7 us
  Pallas kernels  79.1 us (97%)
  local copies, waits for them, and re-layouts  1.98 us (2%)
    pallas_call x1, Pallas kernels, on_device(): pl.pallas_call(kernel, out_shape=(pltpu.VMEM((NFREQ * 64, 512), F32), plt...  79.1 us
    unnamed x2, local copies, waits for them, and re-layouts  1.98 us

profile of v2, /device:TPU:4, one launch (start us, length us, event | category | flops | bytes accessed | tf_op | source)
XLA Modules:
  0.0 81.7 jit_solution(16835609110659101151)
XLA Ops:
  0.6 79.1 %shard_map.59 = (f32[1024,512]{1,0:T(8,128)S(1)}, bf16[64,1024]{1,0:T(8,128)(2,1)S(1)}) custom-call(bf16[768,2048]{1,0:T(8,128)(2,1)} %basis_hbm.1, bf16[768,1024]{1,0:T(8,128)(2,1)} %dens_hbm.1, f32[1,1024]{1,0:T(1,128)} %bitcast.3, f32[16]{0:T(128)} %freq.1), custom_call_target="tpu_custom_call" | custom-call | tf_op jit(solution)/shard_map/pallas_call | solution.py:537
  79.7 1.3 %copy.8 = f32[16,64,512]{2,1,0:T(8,128)} copy(f32[16,64,512]{2,1,0:T(8,128)S(1)} %bitcast.2) | data formatting | bytes 4194304
  81.1 0.7 copy.9

commit v3 on v2

--- a/solution.py
+++ b/solution.py
@@ -15,11 +15,11 @@
 NP = 1024
 NFREQ = 16
 PAIRS = 4096
-NBT = 2
+NBT = 4
 W = NP // NBT
 H = W // 2
-Q = W // 4
-NSEM = 160
+HALF = 256
+NSEM = 3 + NBT * 32
 
 
 def device(x, z, yh, yl, c):
@@ -77,7 +77,7 @@
 
     def copy_to(src, dst, sem, to, recv=None):
         return pltpu.make_async_remote_copy(
-            src_ref=src, dst_ref=dst, send_sem=send_sem.at[sem],
+            src_ref=src, dst_ref=dst, send_sem=send_sem.at[0],
             recv_sem=recv_sem.at[sem] if recv is None else recv,
             device_id=to, device_id_type=MESH,
         )
@@ -124,7 +124,7 @@
     def first_start(b, axis):
         h = 0 if axis == "x" else 1
         me, lo = here[axis], b * W + h * H
-        sems = [slot() for _ in range(6)]
+        sems = [slot() for _ in range(3)]
         far, near = s1_far.at[b, h], s1_near.at[b, h]
         if b == 1 and axis == "x":
             loads[5].wait()
@@ -133,8 +133,8 @@
                 loads[n + 2].wait()
                 turn((x + d) % 4, (z + 2) % 4)
         value = block(axis, (me + 2) % 4, lo, H).astype(BF16)
-        far[0] = value[:, :Q]
-        far[1] = value[:, Q:]
+        far[0] = value[:HALF]
+        far[1] = value[HALF:]
         recv = s1_recv.at[b, h]
         copies = [
             send(far.at[0], recv.at[0], sems[0], along(axis, 1)),
@@ -148,13 +148,13 @@
         sems, copies = sem1[b, axis]
         near, recv = s1_near.at[b, h], s1_recv.at[b, h]
         value = block(axis, (me + 1) % 4, lo, H)
-        near[1] = value[:, Q:].astype(BF16)
-        copies.append(send(near.at[1], recv.at[3], sems[3], along(axis, 1)))
-        own_f32[b, h, 0] = value[:, :Q]
+        near[1] = value[HALF:].astype(BF16)
+        copies.append(send(near.at[1], recv.at[3], sems[2], along(axis, 1)))
+        own_f32[b, h, 0] = value[:HALF]
         value = block(axis, (me + 3) % 4, lo, H)
-        near[2] = value[:, :Q].astype(BF16)
-        copies.append(send(near.at[2], recv.at[4], sems[4], along(axis, 3)))
-        own_f32[b, h, 1] = value[:, Q:]
+        near[2] = value[:HALF].astype(BF16)
+        copies.append(send(near.at[2], recv.at[4], sems[2], along(axis, 3)))
+        own_f32[b, h, 1] = value[HALF:]
 
     def first_own(b, axis):
         h = 0 if axis == "x" else 1
@@ -170,16 +170,16 @@
         copies.append(send(near.at[0], recv.at[2], sems[2], along(axis, 1)))
         copies[1].wait_recv()
         near[3] = (own_f32[b, h, 1] + recv[1].astype(F32)).astype(BF16)
-        copies.append(send(near.at[3], recv.at[5], sems[5], along(axis, 3)))
+        copies.append(send(near.at[3], recv.at[5], sems[2], along(axis, 3)))
 
     def first_end(b, axis):
         h = 0 if axis == "x" else 1
         recv = s1_recv.at[b, h]
-        for cp in sem1[b, axis][1][2:]:
-            cp.wait_recv()
+        last = recv.at[pl.ds(2, 4)]
+        copy_to(last, last, sem1[b, axis][0][2], along(axis, 1)).wait_recv()
         total = s1_sum.at[b, h]
-        total[:, :Q] = total[:, :Q] + recv[2].astype(F32) + recv[4].astype(F32)
-        total[:, Q:] = total[:, Q:] + recv[3].astype(F32) + recv[5].astype(F32)
+        total[:HALF] = total[:HALF] + recv[2].astype(F32) + recv[4].astype(F32)
+        total[HALF:] = total[HALF:] + recv[3].astype(F32) + recv[5].astype(F32)
 
     sem2 = {}
 
@@ -187,15 +187,12 @@
         h = 0 if axis == "x" else 1
         other = "z" if axis == "x" else "x"
         me = here[other]
-        sems = [slot() for _ in range(3)]
-        copies = []
+        sem = slot()
         for i, d in enumerate((2, 1, 3)):
             start = pl.multiple_of((me + d) % 4 * 128, 128)
             s2_send[b, h, i] = s1_sum[b, h, pl.ds(start, 128), :].astype(BF16)
-            copies.append(
-                send(s2_send.at[b, h, i], s2_recv.at[b, h, i], sems[i], along(other, d))
-            )
-        sem2[b, axis] = copies
+            send(s2_send.at[b, h, i], s2_recv.at[b, h, i], sem, along(other, d))
+        sem2[b, axis] = sem
 
     is_home = g == x
     is_source = is_home
@@ -207,15 +204,15 @@
     out2_to = device((g + 2) % 4, z, yh, yl, c)
 
     def split(b):
-        return b == 0
+        return b in (1, 2)
 
     sem_y = {}
 
     def second_end(b, axis):
         h = 0 if axis == "x" else 1
         other = "z" if axis == "x" else "x"
-        for cp in sem2[b, axis]:
-            cp.wait_recv()
+        every = s2_recv.at[b, h]
+        copy_to(every, every, sem2[b, axis], along(other, 1)).wait_recv()
         start = pl.multiple_of(here[other] * 128, 128)
         total = s1_sum[b, h, pl.ds(start, 128), :]
         for i in range(3):
@@ -238,13 +235,13 @@
             cond = yl != yh if h == 1 and split(b) else None
             pair = (ib.at[b, g, h], jb.at[b, z, h, g, own_rows])
             if cond is None:
-                send(*pair, slot(), other_home, recv=home_sem.at[b, h, g])
+                send(*pair, 0, other_home, recv=home_sem.at[b, h])
             else:
-                send_if(cond, *pair, slot(), other_home, recv=home_sem.at[b, h, g])
+                send_if(cond, *pair, 0, other_home, recv=home_sem.at[b, h])
         mine = ib.at[b, g]
         send_if(
-            g != x, mine, mine, slot(), device(x, z, yh, x // 2, x % 2),
-            recv=row_sem.at[b, (x - g + 4) % 4],
+            g != x, mine, mine, 0, device(x, z, yh, x // 2, x % 2),
+            recv=row_sem.at[b],
         )
 
     def rows_more(b):
@@ -252,14 +249,13 @@
         for d in range(1, 4):
             o = (g + d) % 4
             send_if(
-                o != x, mine, mine, slot(), device(x, z, yh, o // 2, o % 2),
-                recv=row_sem.at[b, d],
+                o != x, mine, mine, 0, device(x, z, yh, o // 2, o % 2),
+                recv=row_sem.at[b],
             )
 
     def rows_end(b):
-        for d in range(1, 4):
-            o = (g - d + 4) % 4
-            copy_to(ib.at[b, o], ib.at[b, o], 0, along("x", 1), recv=row_sem.at[b, d]).wait_recv()
+        three = ib.at[b, pl.ds(0, 3)]
+        copy_to(three, three, 0, along("x", 1), recv=row_sem.at[b]).wait_recv()
 
     def weigh(b):
         if b == 0:
@@ -278,18 +274,16 @@
     def scale(b):
         pl.when(jnp.logical_not(is_home))(lambda: rows_end(b))
         for h in range(2):
-            for gg in range(4):
-                sl = slice(gg * H, (gg + 1) * H)
-                rows = ib[b, gg, h].astype(F32)
-
-                def at(k, _, h=h, sl=sl, rows=rows):
-                    start = pl.multiple_of(k * 64, 64)
-                    scaled[b, h, pl.ds(start, 64), sl] = (
-                        wts[b, h, pl.ds(k, 1), sl] * rows
-                    ).astype(BF16)
-                    return 0
-
-                lax.fori_loop(0, NFREQ, at, 0)
+            rows = jnp.concatenate([ib[b, gg, h] for gg in range(4)], axis=1).astype(F32)
+
+            def at(k, _, h=h, rows=rows):
+                start = pl.multiple_of(k * 64, 64)
+                scaled[b, h, pl.ds(start, 64), :] = (
+                    wts[b, h, pl.ds(k, 1), :] * rows
+                ).astype(BF16)
+                return 0
+
+            lax.fori_loop(0, NFREQ, at, 0)
 
     sem_g = {}
     zn = [z, (z + 3) % 4, (z + 1) % 4, (z + 2) % 4]
@@ -313,14 +307,12 @@
         return [half(b, zz, h, n) for n in range(2)]
 
     def gather1(b):
-        ss = {name + str(h): slot() for name in ("a0", "a1", "b0", "b1", "c", "d") for h in range(2)}
+        ss = {name + str(h): slot() for name in ("a0", "ab", "b1", "c", "d") for h in range(2)}
         for n in range(2):
             ss["x1", n] = slot()
-            ss["x1o", n] = slot()
         for i in range(4):
             for n in range(1 if split(b) else 2):
                 ss["x2", i, n] = slot()
-                ss["x2o", i, n] = slot()
             if split(b):
                 ss["y2", i] = slot()
         sem_g[b] = ss
@@ -332,16 +324,14 @@
                 groups = [2 * yh, 2 * yh + 1] if h == 1 and split(b) else range(4)
                 for gg in groups:
                     jb[b, z, h, gg, own_rows, :] = ib[b, gg, h]
-                for gg in groups:
-                    block = jb.at[b, z, h, gg, own_rows]
-                    copy_to(block, block, 0, along("x", 1), recv=home_sem.at[b, h, gg]).wait_recv()
+                block = jb.at[b, z, h, pl.ds(0, len(groups)), own_rows]
+                copy_to(block, block, 0, along("x", 1), recv=home_sem.at[b, h]).wait_recv()
 
             if h == 0:
                 for n, piece in enumerate(pieces(b, z, 0)):
                     send_if(is_source, piece, piece, ss["x1", n], out1_to)
                     send_if(
-                        is_source, piece, piece, ss["x1o", n], pair_to,
-                        recv=recv_sem.at[ss["x1", n]],
+                        is_source, piece, piece, ss["x1", n], pair_to
                     )
             else:
                 ring_start(b, 1, is_source)
@@ -350,8 +340,8 @@
         ss = sem_g[b]
         for n in range(2):
             up, down = half(b, z, h, n), half(b, z, h, 1 - n)
-            one = (up, up, ss[f"a{n}{h}"], along("z", 1))
-            two = (down, down, ss[f"b{1 - n}{h}"], along("z", 3))
+            one = (up, up, ss[("a0", "ab")[n] + str(h)], along("z", 1))
+            two = (down, down, ss[("b1", "ab")[n] + str(h)], along("z", 3))
             for args in (one, two):
                 if cond is None:
                     send(*args)
@@ -378,8 +368,7 @@
             if which is None or n == which:
                 send_if(is_source, piece, piece, ss["x2", i, n], out1_to)
                 send_if(
-                    is_source, piece, piece, ss["x2o", i, n], pair_to,
-                    recv=recv_sem.at[ss["x2", i, n]],
+                    is_source, piece, piece, ss["x2", i, n], pair_to
                 )
 
     def pass2(b, i):
@@ -414,9 +403,7 @@
                 send(ref, ref, ss[f"{on}{h}"], along("z", d))
             else:
                 send_if(cond, ref, ref, ss[f"{on}{h}"], along("z", d))
-        for i, n, name in ((1, 1, "a1"), (2, 0, "b0")):
-            ref = half(b, zn[i], h, n)
-            under(cond, lambda ref=ref, name=name: wait_in(ref, ss[f"{name}{h}"], along("z", 1)))
+        under(cond, lambda: wait_in(part(b, zn[1], h), ss[f"ab{h}"], along("z", 1)))
 
     def ring_end(b, h, cond, after=None):
         ss = sem_g[b]
@@ -475,12 +462,12 @@
             turn((x + d) % 4, (z + e) % 4)
     near_part(0, 'x')
     near_part(0, 'z')
-    first_start(1, 'x')
-    first_start(1, 'z')
     first_own(0, 'x')
     first_own(0, 'z')
     first_forward(0, 'x')
     first_forward(0, 'z')
+    first_start(1, 'x')
+    first_start(1, 'z')
     near_part(1, 'x')
     near_part(1, 'z')
     first_own(1, 'x')
@@ -489,42 +476,96 @@
     first_end(0, 'z')
     second_start(0, 'x')
     second_start(0, 'z')
+    weigh(0)
     first_forward(1, 'x')
     first_forward(1, 'z')
-    weigh(0)
-    weigh(1)
+    first_start(2, 'x')
+    first_start(2, 'z')
+    near_part(2, 'x')
+    near_part(2, 'z')
+    first_own(2, 'x')
+    first_own(2, 'z')
     second_end(0, 'x')
     second_end(0, 'z')
     first_end(1, 'x')
     first_end(1, 'z')
     second_start(1, 'x')
     second_start(1, 'z')
+    weigh(1)
+    first_forward(2, 'x')
+    first_forward(2, 'z')
+    first_start(3, 'x')
+    first_start(3, 'z')
+    near_part(3, 'x')
+    near_part(3, 'z')
+    first_own(3, 'x')
+    first_own(3, 'z')
     rows_start(0)
     second_end(1, 'x')
     second_end(1, 'z')
+    first_end(2, 'x')
+    first_end(2, 'z')
+    second_start(2, 'x')
+    second_start(2, 'z')
+    weigh(2)
+    first_forward(3, 'x')
+    first_forward(3, 'z')
     gather1(0)
     rows_start(1)
+    second_end(2, 'x')
+    second_end(2, 'z')
+    first_end(3, 'x')
+    first_end(3, 'z')
+    second_start(3, 'x')
+    second_start(3, 'z')
+    weigh(3)
     gather2(0)
     rows_more(0)
+    rows_start(2)
     gather1(1)
+    second_end(3, 'x')
+    second_end(3, 'z')
     gather3(0)
+    scale(0)
     gather2(1)
     rows_more(1)
+    rows_start(3)
     gather4(0)
-    scale(0)
+    gather1(2)
+    multiply(0, 0, (0, 1), first=True)
     gather3(1)
-    multiply(0, 0, (0, 1), first=True)
     gather5(0)
     scale(1)
+    gather2(2)
     multiply(0, 0, (2, 3), first=True)
+    multiply(0, 1, (0, 1))
+    rows_more(2)
     gather4(1)
-    multiply(0, 1, (0, 1))
+    gather1(3)
+    multiply(1, 0, (0, 1))
+    gather3(2)
     multiply(0, 1, (2, 3))
-    multiply(1, 0, (0, 1))
+    gather5(1)
+    scale(2)
+    gather2(3)
+    multiply(1, 0, (2, 3))
     multiply(1, 1, (0, 1))
-    gather5(1)
-    multiply(1, 0, (2, 3))
+    rows_more(3)
+    gather4(2)
+    multiply(2, 0, (0, 1))
+    gather3(3)
     multiply(1, 1, (2, 3))
+    gather5(2)
+    scale(3)
+    multiply(2, 0, (2, 3))
+    multiply(2, 1, (0, 1))
+    gather4(3)
+    multiply(3, 0, (0, 1))
+    multiply(2, 1, (2, 3))
+    gather5(3)
+    multiply(3, 0, (2, 3))
+    multiply(3, 1, (0, 1))
+    multiply(3, 1, (2, 3))
     for cond, cp in drains:
         if cond is None:
             cp.wait_send()
@@ -546,10 +587,10 @@
             pltpu.VMEM((NK, NB), BF16),
             pltpu.VMEM((NK, NP), BF16),
             pltpu.VMEM((4, 4, 128, NK), BF16),
-            pltpu.VMEM((NBT, 2, 2, 512, Q), F32),
-            pltpu.VMEM((NBT, 2, 6, 512, Q), BF16),
-            pltpu.VMEM((NBT, 2, 2, 512, Q), BF16),
-            pltpu.VMEM((NBT, 2, 4, 512, Q), BF16),
+            pltpu.VMEM((NBT, 2, 2, HALF, H), F32),
+            pltpu.VMEM((NBT, 2, 6, HALF, H), BF16),
+            pltpu.VMEM((NBT, 2, 2, HALF, H), BF16),
+            pltpu.VMEM((NBT, 2, 4, HALF, H), BF16),
             pltpu.VMEM((NBT, 2, 512, H), F32),
             pltpu.VMEM((NBT, 2, 3, 128, H), BF16),
             pltpu.VMEM((NBT, 2, 3, 128, H), BF16),
@@ -562,10 +603,10 @@
             pltpu.VMEM((NBT, 2, NFREQ * 64, 2 * W), BF16),
             pltpu.VMEM((NBT, 4, 2, 4, 128, H), BF16),
             pltpu.SemaphoreType.DMA((6,)),
+            pltpu.SemaphoreType.DMA((1,)),
             pltpu.SemaphoreType.DMA((NSEM,)),
-            pltpu.SemaphoreType.DMA((NSEM,)),
-            pltpu.SemaphoreType.DMA((NBT, 2, 4)),
-            pltpu.SemaphoreType.DMA((NBT, 4)),
+            pltpu.SemaphoreType.DMA((NBT, 2)),
+            pltpu.SemaphoreType.DMA((NBT,)),
         ],
         compiler_params=pltpu.CompilerParams(
             collective_id=0, has_side_effects=True, vmem_limit_bytes=56 * 2**20

time: 81.9 us -> 77.1 us (0.941)
  Pallas kernels: 79.1 us -> 74.3 us
    pallas_call x1, Pallas kernels: 79.1 us -> 74.3 us  [on_device(): pl.pallas_call(kernel, out_shape=(pltpu.VMEM((NFREQ * 64, 512), F32), plt...]
where the time goes in v3:
time: 77.1 us; the launch traced here: 76.9 us
  Pallas kernels  74.3 us (96%)
  local copies, waits for them, and re-layouts  1.98 us (3%)
    pallas_call x1, Pallas kernels, on_device(): pl.pallas_call(kernel, out_shape=(pltpu.VMEM((NFREQ * 64, 512), F32), plt...  74.3 us
    unnamed x2, local copies, waits for them, and re-layouts  1.98 us

profile of v3, /device:TPU:4, one launch (start us, length us, event | category | flops | bytes accessed | tf_op | source)
XLA Modules:
  0.0 76.9 jit_solution(12838088258392860377)
XLA Ops:
  0.6 74.3 %shard_map.59 = (f32[1024,512]{1,0:T(8,128)S(1)}, bf16[64,1024]{1,0:T(8,128)(2,1)S(1)}) custom-call(bf16[768,2048]{1,0:T(8,128)(2,1)} %basis_hbm.1, bf16[768,1024]{1,0:T(8,128)(2,1)} %dens_hbm.1, f32[1,1024]{1,0:T(1,128)} %bitcast.3, f32[16]{0:T(128)} %freq.1), custom_call_target="tpu_custom_call" | custom-call | tf_op jit(solution)/shard_map/pallas_call | solution.py:578
  74.9 1.3 %copy.8 = f32[16,64,512]{2,1,0:T(8,128)} copy(f32[16,64,512]{2,1,0:T(8,128)S(1)} %bitcast.2) | data formatting | bytes 4194304
  76.3 0.7 copy.9

commit v4 on v3

--- a/solution.py
+++ b/solution.py
@@ -285,6 +285,9 @@
 
             lax.fori_loop(0, NFREQ, at, 0)
 
+    def direct(b):
+        return b == NBT - 1
+
     sem_g = {}
     zn = [z, (z + 3) % 4, (z + 1) % 4, (z + 2) % 4]
 
@@ -330,6 +333,8 @@
             if h == 0:
                 for n, piece in enumerate(pieces(b, z, 0)):
                     send_if(is_source, piece, piece, ss["x1", n], out1_to)
+                    if direct(b):
+                        send_if(is_source, piece, piece, ss["x1", n], out2_to)
                     send_if(
                         is_source, piece, piece, ss["x1", n], pair_to
                     )
@@ -356,9 +361,8 @@
             def _(n=n, piece=piece):
                 wait_in(piece, ss["x1", n], along("x", 1))
 
-            fwd = copy_to(piece, piece, ss["x1", n], out2_to)
-            pl.when(is_out1)(fwd.start)
-            drains.append((is_out1, fwd))
+            if not direct(b):
+                send_if(is_out1, piece, piece, ss["x1", n], out2_to)
         ring_start(b, 0, None)
         spread2(b, 0)
 
@@ -367,6 +371,8 @@
         for n, piece in enumerate(pieces(b, zn[i], 1)):
             if which is None or n == which:
                 send_if(is_source, piece, piece, ss["x2", i, n], out1_to)
+                if direct(b):
+                    send_if(is_source, piece, piece, ss["x2", i, n], out2_to)
                 send_if(
                     is_source, piece, piece, ss["x2", i, n], pair_to
                 )
@@ -379,9 +385,8 @@
             def _(n=n, piece=piece):
                 wait_in(piece, ss["x2", i, n], along("x", 1))
 
-            fwd = copy_to(piece, piece, ss["x2", i, n], out2_to)
-            pl.when(is_out1)(fwd.start)
-            drains.append((is_out1, fwd))
+            if not direct(b):
+                send_if(is_out1, piece, piece, ss["x2", i, n], out2_to)
         if split(b):
             send(piece, piece, ss["y2", i], beside(4))
 
@@ -417,8 +422,8 @@
         ring_mid(b, 1, is_source)
         spread2(b, 1)
         spread2(b, 2)
+        pass2(b, 0)
         ring_mid(b, 0, None)
-        pass2(b, 0)
 
     def gather4(b):
         if split(b):
@@ -430,8 +435,8 @@
         pass2(b, 2)
 
     def gather5(b):
+        pass2(b, 3)
         ring_end(b, 0, None)
-        pass2(b, 3)
 
     def multiply(b, h, which, first=False):
         if h == 1 and split(b):

time: 77.1 us -> 75.4 us (0.978)
  Pallas kernels: 74.3 us -> 72.6 us
    pallas_call x1, Pallas kernels: 74.3 us -> 72.6 us  [on_device(): pl.pallas_call(kernel, out_shape=(pltpu.VMEM((NFREQ * 64, 512), F32), plt...]
where the time goes in v4:
time: 75.4 us; the launch traced here: 75.2 us
  Pallas kernels  72.6 us (96%)
  local copies, waits for them, and re-layouts  1.98 us (3%)
    pallas_call x1, Pallas kernels, on_device(): pl.pallas_call(kernel, out_shape=(pltpu.VMEM((NFREQ * 64, 512), F32), plt...  72.6 us
    unnamed x2, local copies, waits for them, and re-layouts  1.98 us

profile of v4, /device:TPU:4, one launch (start us, length us, event | category | flops | bytes accessed | tf_op | source)
XLA Modules:
  0.0 75.2 jit_solution(3081084574717595353)
XLA Ops:
  0.6 72.6 %shard_map.59 = (f32[1024,512]{1,0:T(8,128)S(1)}, bf16[64,1024]{1,0:T(8,128)(2,1)S(1)}) custom-call(bf16[768,2048]{1,0:T(8,128)(2,1)} %basis_hbm.1, bf16[768,1024]{1,0:T(8,128)(2,1)} %dens_hbm.1, f32[1,1024]{1,0:T(1,128)} %bitcast.3, f32[16]{0:T(128)} %freq.1), custom_call_target="tpu_custom_call" | custom-call | tf_op jit(solution)/shard_map/pallas_call | solution.py:583
  73.2 1.3 %copy.8 = f32[16,64,512]{2,1,0:T(8,128)} copy(f32[16,64,512]{2,1,0:T(8,128)S(1)} %bitcast.2) | data formatting | bytes 4194304
  74.5 0.7 copy.9

commit v5 on v4

--- a/solution.py
+++ b/solution.py
@@ -567,9 +567,10 @@
     gather4(3)
     multiply(3, 0, (0, 1))
     multiply(2, 1, (2, 3))
-    gather5(3)
+    multiply(3, 1, (0, 1))
+    ring_end(3, 0, None)
     multiply(3, 0, (2, 3))
-    multiply(3, 1, (0, 1))
+    pass2(3, 3)
     multiply(3, 1, (2, 3))
     for cond, cp in drains:
         if cond is None:

time: 75.4 us -> 75.6 us (level)
  no operation moved by 1% of the time
where the time goes in v5:
time: 75.6 us; the launch traced here: 75.4 us
  Pallas kernels  72.8 us (96%)
  local copies, waits for them, and re-layouts  1.98 us (3%)
    pallas_call x1, Pallas kernels, on_device(): pl.pallas_call(kernel, out_shape=(pltpu.VMEM((NFREQ * 64, 512), F32), plt...  72.8 us
    unnamed x2, local copies, waits for them, and re-layouts  1.98 us

profile of v5, /device:TPU:4, one launch (start us, length us, event | category | flops | bytes accessed | tf_op | source)
XLA Modules:
  0.0 75.4 jit_solution(18290272040808437076)
XLA Ops:
  0.6 72.8 %shard_map.59 = (f32[1024,512]{1,0:T(8,128)S(1)}, bf16[64,1024]{1,0:T(8,128)(2,1)S(1)}) custom-call(bf16[768,2048]{1,0:T(8,128)(2,1)} %basis_hbm.1, bf16[768,1024]{1,0:T(8,128)(2,1)} %dens_hbm.1, f32[1,1024]{1,0:T(1,128)} %bitcast.3, f32[16]{0:T(128)} %freq.1), custom_call_target="tpu_custom_call" | custom-call | tf_op jit(solution)/shard_map/pallas_call | solution.py:584
  73.5 1.3 %copy.8 = f32[16,64,512]{2,1,0:T(8,128)} copy(f32[16,64,512]{2,1,0:T(8,128)S(1)} %bitcast.2) | data formatting | bytes 4194304
  74.8 0.7 copy.9
